TPU v7x, 32 devices: a whole 2x2x4 slice. The times are simulated.
32 devices in a mesh: src: 8 (over z, x), att: 4 (over y, core).
Axes of the slice: x: 2, y: 2, z: 4, core: 2. Of those that a mesh axis runs over, the one named last changes fastest.
Arguments:
- residual: float32 [262144], P(('src', 'att')), may hold values from -6 to 6
- weight: float32 [262144], P(('src', 'att')), may hold values from 0.2 to 5
- source_part: float32 [5, 262144], P(None, ('src', 'att')), may hold values from -6 to 6
- attitude_part: float32 [4, 262144], P(None, ('src', 'att')), may hold values from -6 to 6
- calib_part: float32 [262144], P(('src', 'att')), may hold values from -6 to 6
- phase: float32 [262144], P(('src', 'att')), may hold values from 0 to 1
- obs_source: int32 [262144], P(('src', 'att')), may hold values from 0 to 63
- obs_owner: int32 [262144], P(('src', 'att')), may hold values from 0 to 31
- obs_slot: int32 [262144], P(('src', 'att')), may hold values from 0 to 3
- obs_knot: int32 [262144], P(('src', 'att')), may hold values from 0 to 124
- obs_calib: int32 [262144], P(('src', 'att')), may hold values from 0 to 2047
- tile_count: int32 [32, 4], P(('src', 'att')), may hold values from 1 to 2048, 5120 in all within a row
- time_list: int32 [32, 32, 4], P(None, ('src', 'att')), may hold values from 0 to 7
Outputs:
- source_update: float32 [5, 8192], P(None, ('src', 'att'))
- attitude_update: float32 [4, 32768], P(None, ('src', 'att'))
- calib_update: float32 [2048], replicated
- residual_out: float32 [262144], P(('src', 'att'))
Inputs may be any that keep to these rules, and one draw needn't show every extreme that they name: `tile_count`: each device's tile counts sum to 5120. `time_list`: local knot block of the owner; entries may repeat.
All inputs are finite; a program needn't handle non-finite values.
Results may differ from a plain program's by a relative error of at most 0.0001.
Values sent between devices are 32-bit elements; how exact they have to be, the bound alone decides.
A program may use at most 64 MiB of HBM per device.

v0:
```python
import math

import jax
import jax.numpy as jnp
from jax import lax
from jax.sharding import PartitionSpec as P

OBS_TILE = 2048
SRC_TILE = 64
KNOT = 128
LIST = 4
KB_DEV = 8
NCAL = 2048


HIGH = lax.Precision.HIGHEST


def spline_weights(phase):
    other = 1.0 - phase
    square = phase * phase
    cube = square * phase
    return [
        other * other * other / 6.0,
        (3.0 * cube - 6.0 * square + 4.0) / 6.0,
        (-3.0 * cube + 3.0 * square + 3.0 * phase + 1.0) / 6.0,
        cube / 6.0,
    ]


def solve_normals(sums):
    matrix = [[None] * 5 for _ in range(5)]
    column = 0
    for left in range(5):
        for right in range(left, 5):
            matrix[left][right] = sums[:, column]
            matrix[right][left] = sums[:, column]
            column += 1
    target = [sums[:, 15 + left] for left in range(5)]
    for left in range(5):
        matrix[left][left] = matrix[left][left] + 1.0
    for pivot in range(5):
        for lower in range(pivot + 1, 5):
            factor = matrix[lower][pivot] / matrix[pivot][pivot]
            for right in range(pivot, 5):
                matrix[lower][right] = matrix[lower][right] - factor * matrix[pivot][right]
            target[lower] = target[lower] - factor * target[pivot]
    result = [None] * 5
    for pivot in range(4, -1, -1):
        value = target[pivot]
        for right in range(pivot + 1, 5):
            value = value - matrix[pivot][right] * result[right]
        result[pivot] = value / matrix[pivot][pivot]
    return jnp.stack(result, 0)


def knot_rows(basis_rows, knot_first, squared):
    knots = knot_first.shape[0]
    positions = jnp.arange(KNOT, dtype=jnp.int32)[None, :]
    total = jnp.zeros((knots, KNOT), jnp.float32)
    for offset in range(4):
        value = basis_rows[:, offset]
        if squared:
            value = value * value
        total = total + jnp.where(
            positions == knot_first[:, None] + offset, value[:, None], jnp.float32(0.0)
        )
    return total


def on_device(
    residual,
    weight,
    source_part,
    attitude_part,
    calib_part,
    phase,
    obs_source,
    obs_owner,
    obs_slot,
    obs_knot,
    obs_calib,
    tile_count,
    time_list,
):
    count = residual.shape[0]
    devices = lax.axis_size(("src", "att"))
    tiles = tile_count.shape[1]
    index = jnp.arange(count, dtype=jnp.int32)
    live = (index % OBS_TILE).reshape(tiles, OBS_TILE) < tile_count.reshape(tiles, 1)
    weighted = jnp.where(live.reshape(count), weight, jnp.float32(0.0))
    onehot = (
        obs_source.reshape(tiles, OBS_TILE)[:, :, None]
        == jnp.arange(SRC_TILE, dtype=jnp.int32)[None, None, :]
    ).astype(jnp.float32)
    columns = []
    for left in range(5):
        for right in range(left, 5):
            columns.append(weighted * source_part[left] * source_part[right])
    for left in range(5):
        columns.append(weighted * source_part[left] * residual)
    stacked = jnp.stack(columns, 0).reshape(20, tiles, OBS_TILE)
    sums = jnp.einsum(
        "tos,cto->tsc", onehot, stacked, precision=HIGH, preferred_element_type=jnp.float32
    )
    source_update = solve_normals(sums.reshape(tiles * SRC_TILE, 20))
    per_obs = jnp.einsum(
        "tos,kts->kto",
        onehot,
        source_update.reshape(5, tiles, SRC_TILE),
        precision=HIGH,
        preferred_element_type=jnp.float32,
    )
    first = residual - jnp.sum(source_part * per_obs.reshape(5, count), axis=0)
    basis_rows = jnp.stack(spline_weights(phase), 1)
    attitude_rows = attitude_part.T
    listed_blocks = devices * LIST
    block_id = obs_owner * LIST + obs_slot
    rhs_terms = weighted[:, None] * attitude_rows * first[:, None]
    diag_terms = weighted[:, None] * attitude_rows * attitude_rows
    calib_terms_obs = jnp.stack(
        [weighted * calib_part * first, weighted * calib_part * calib_part], 1
    )
    step_rows = math.gcd(count, 2048)
    steps = count // step_rows
    block_ids = jnp.arange(listed_blocks, dtype=jnp.int32)[None, :]
    calib_ids = jnp.arange(NCAL, dtype=jnp.int32)[None, :]

    def accumulate(carry, inputs):
        partial_value, calib_sum = carry
        blocks, knot_first, basis_part, rhs_part, diag_part, calib_ids_part, calib_vals = inputs
        linear = knot_rows(basis_part, knot_first, False)
        squares = knot_rows(basis_part, knot_first, True)
        spread = jnp.concatenate(
            [
                linear[:, :, None] * rhs_part[:, None, :],
                squares[:, :, None] * diag_part[:, None, :],
            ],
            axis=2,
        )
        spread = spread.reshape(step_rows, KNOT * 8)
        selector = (blocks[:, None] == block_ids).astype(jnp.float32)
        partial_value = partial_value + jnp.einsum(
            "ib,im->bm", selector, spread, precision=HIGH, preferred_element_type=jnp.float32
        )
        calib_hot = (calib_ids_part[:, None] == calib_ids).astype(jnp.float32)
        calib_sum = calib_sum + jnp.einsum(
            "in,ic->cn", calib_hot, calib_vals, precision=HIGH, preferred_element_type=jnp.float32
        )
        return ((partial_value, calib_sum), None)

    inputs = (
        block_id.reshape(steps, step_rows),
        obs_knot.reshape(steps, step_rows),
        basis_rows.reshape(steps, step_rows, 4),
        rhs_terms.reshape(steps, step_rows, 4),
        diag_terms.reshape(steps, step_rows, 4),
        obs_calib.reshape(steps, step_rows),
        calib_terms_obs.reshape(steps, step_rows, 2),
    )
    start = (jnp.zeros((listed_blocks, KNOT * 8), jnp.float32), jnp.zeros((2, NCAL), jnp.float32))
    (partial_value, calib_terms), _ = lax.scan(accumulate, start, inputs)
    outgoing = partial_value.reshape(devices, LIST, KNOT * 8)
    arrived = lax.all_to_all(outgoing, ("src", "att"), split_axis=0, concat_axis=0, tiled=True)
    totals = lax.psum(calib_terms, ("src", "att"))
    calib_update = totals[0] / (totals[1] + 1.0)
    listed = time_list.reshape(devices * LIST)
    selector = (listed[None, :] == jnp.arange(KB_DEV, dtype=jnp.int32)[:, None]).astype(jnp.float32)
    owned = jnp.dot(
        selector,
        arrived.reshape(devices * LIST, KNOT * 8),
        precision=HIGH,
        preferred_element_type=jnp.float32,
    )
    owned = owned.reshape(KB_DEV, KNOT, 8)
    update = owned[:, :, 0:4] / (owned[:, :, 4:8] + 1.0)
    attitude_update = update.reshape(KB_DEV * KNOT, 4).T
    returning = jnp.dot(
        selector.T,
        update.reshape(KB_DEV, KNOT * 4),
        precision=HIGH,
        preferred_element_type=jnp.float32,
    )
    returning = returning.reshape(devices, LIST, KNOT * 4)
    segment = lax.all_to_all(returning, ("src", "att"), split_axis=0, concat_axis=0, tiled=True)
    segment_rows = segment.reshape(listed_blocks, KNOT * 4)

    def correct(carry, inputs):
        blocks, knot_first, basis_part, attitude_block, calib_ids_part, calib_coef, first_part = (
            inputs
        )
        selector_rows = (blocks[:, None] == block_ids).astype(jnp.float32)
        fetched = jnp.dot(
            selector_rows, segment_rows, precision=HIGH, preferred_element_type=jnp.float32
        )
        fetched = fetched.reshape(step_rows, KNOT, 4)
        projected = jnp.sum(fetched * attitude_block[:, None, :], axis=2)
        linear = knot_rows(basis_part, knot_first, False)
        attitude_term = jnp.sum(linear * projected, axis=1)
        calib_hot = (calib_ids_part[:, None] == calib_ids).astype(jnp.float32)
        calib_value = jnp.dot(
            calib_hot, calib_update, precision=HIGH, preferred_element_type=jnp.float32
        )
        return (carry, first_part - attitude_term - calib_coef * calib_value)

    inputs_back = (
        block_id.reshape(steps, step_rows),
        obs_knot.reshape(steps, step_rows),
        basis_rows.reshape(steps, step_rows, 4),
        attitude_rows.reshape(steps, step_rows, 4),
        obs_calib.reshape(steps, step_rows),
        calib_part.reshape(steps, step_rows),
        first.reshape(steps, step_rows),
    )
    _, residual_blocks = lax.scan(correct, jnp.float32(0.0), inputs_back)
    residual_out = residual_blocks.reshape(count)
    return (source_update, attitude_update, calib_update, residual_out)


def solution(mesh):
    placed = (
        P(("src", "att")),
        P(("src", "att")),
        P(None, ("src", "att")),
        P(None, ("src", "att")),
        P(("src", "att")),
        P(("src", "att")),
        P(("src", "att")),
        P(("src", "att")),
        P(("src", "att")),
        P(("src", "att")),
        P(("src", "att")),
        P(("src", "att"), None),
        P(None, ("src", "att"), None),
    )
    return jax.shard_map(
        on_device,
        mesh=mesh,
        in_specs=placed,
        out_specs=(P(None, ("src", "att")), P(None, ("src", "att")), P(), P(("src", "att"))),
        check_vma=False,
    )
```

profile of v0, /device:TPU:0, one launch (start us, length us, event | category | flops | bytes accessed | tf_op | source)
XLA Modules:
  0.0 256.5 jit_solution(3903458531358402341)
XLA Ops:
  1.4 1.9 fusion.111
  3.3 0.8 eq.285
  4.1 0.8 multiply_multiply_fusion.6
  4.9 0.8 multiply_multiply_fusion.8
  5.7 1.0 stack.117
  6.7 1.1 fusion.27
  9.9 0.7 fusion.26
  11.1 87.2 %while.25 = (s32[]{:T(128)}, f32[128,1024]{1,0:T(8,128)S(1)}, f32[2,2048]{1,0:T(2,128)S(1)}, s32[4,2048]{1,0:T(4,128)S(1)}, s32[4,2048]{1,0:T(4,128)S(1)}, /*ind...) while((s32[]{:T(128)}, f32[128,1024]{1,0:T(8,128)S(1)}, ...), condition=%wide.region_2.3_spmd.clone, body=%wide.region_1.2_spmd.clone.sunk | while | flops 3335804928 | bytes 22626460 | solution.py:162
  12.1 3.1 %broadcast_multiply_fusion.4 = f32[2048,128,4]{0,2,1:T(4,128)} fusion(f32[2048,4]{0,1:T(4,128)S(1)} %get-tuple-element.550, f32[2048,128]{0,1:T(8,128)S(1)} %get-tuple-element.563), kind=kLoop, calls=%fused_computation.35.clone.1 | loop fusion | flops 1048576 | bytes 5275648 | tf_op jit(solution)/shard_map/while/body/eval_jaxpr/mul | solution.py:137
  15.2 3.2 %broadcast_multiply_fusion.5 = f32[2048,128,4]{0,2,1:T(4,128)} fusion(f32[2048,4]{0,1:T(4,128)S(1)} %get-tuple-element.564, f32[2048,128]{0,1:T(8,128)S(1)} %get-tuple-element.565), kind=kLoop, calls=%fused_computation.36.clone.1 | loop fusion | flops 1048576 | bytes 5275648 | tf_op jit(solution)/shard_map/while/body/eval_jaxpr/mul | solution.py:136
  18.4 9.3 %fusion.136 = f32[128,1024]{1,0:T(8,128)S(1)} fusion(f32[2048,128,4]{0,2,1:T(4,128)} %broadcast_multiply_fusion.4, f32[2048,128,4]{0,2,1:T(4,128)} %broadcast_multiply_fusion.5, f32[128,1024]{1,0:T(8,128)S(1)} %get-tuple-element.580, s32[2048]{0:T(1024)S(1)} %bitcast.454, pred[]{:T(512)S(6)} %compare.4), kind=kOutput, calls=%fused_computation.37.clone.1 | convolution fusion | flops 3224109056 | bytes 9445377 | tf_op jit(solution)/shard_map/while/body/eval_jaxpr/ib,im->bm/dot_general | solution.py:143
  27.7 5.4 %fusion.137 = f32[2,2048]{1,0:T(2,128)S(1)} fusion(s32[2048]{0:T(1024)S(1)} %bitcast.470, f32[2,2048]{1,0:T(2,128)S(1)} %get-tuple-element.581, f32[4,2048,2]{1,2,0:T(2,128)S(1)} %get-tuple-element.599, s32[]{:T(128)S(6)} %copy.66, pred[]{:T(512)S(6)} %compare.4), kind=kOutput, calls=%fused_computation.34.clone.1 | convolution fusion | flops 104865792 | bytes 57349 | tf_op jit(solution)/shard_map/while/body/eval_jaxpr/in,ic->cn/dot_general | solution.py:147
  33.8 3.1 %broadcast_multiply_fusion.4 = f32[2048,128,4]{0,2,1:T(4,128)} fusion(f32[2048,4]{0,1:T(4,128)S(1)} %get-tuple-element.550, f32[2048,128]{0,1:T(8,128)S(1)} %get-tuple-element.563), kind=kLoop, calls=%fused_computation.35.clone.1 | loop fusion | flops 1048576 | bytes 5275648 | tf_op jit(solution)/shard_map/while/body/eval_jaxpr/mul | solution.py:137
  36.9 3.2 %broadcast_multiply_fusion.5 = f32[2048,128,4]{0,2,1:T(4,128)} fusion(f32[2048,4]{0,1:T(4,128)S(1)} %get-tuple-element.564, f32[2048,128]{0,1:T(8,128)S(1)} %get-tuple-element.565), kind=kLoop, calls=%fused_computation.36.clone.1 | loop fusion | flops 1048576 | bytes 5275648 | tf_op jit(solution)/shard_map/while/body/eval_jaxpr/mul | solution.py:136
  40.1 9.3 %fusion.136 = f32[128,1024]{1,0:T(8,128)S(1)} fusion(f32[2048,128,4]{0,2,1:T(4,128)} %broadcast_multiply_fusion.4, f32[2048,128,4]{0,2,1:T(4,128)} %broadcast_multiply_fusion.5, f32[128,1024]{1,0:T(8,128)S(1)} %get-tuple-element.580, s32[2048]{0:T(1024)S(1)} %bitcast.454, pred[]{:T(512)S(6)} %compare.4), kind=kOutput, calls=%fused_computation.37.clone.1 | convolution fusion | flops 3224109056 | bytes 9445377 | tf_op jit(solution)/shard_map/while/body/eval_jaxpr/ib,im->bm/dot_general | solution.py:143
  49.4 5.4 %fusion.137 = f32[2,2048]{1,0:T(2,128)S(1)} fusion(s32[2048]{0:T(1024)S(1)} %bitcast.470, f32[2,2048]{1,0:T(2,128)S(1)} %get-tuple-element.581, f32[4,2048,2]{1,2,0:T(2,128)S(1)} %get-tuple-element.599, s32[]{:T(128)S(6)} %copy.66, pred[]{:T(512)S(6)} %compare.4), kind=kOutput, calls=%fused_computation.34.clone.1 | convolution fusion | flops 104865792 | bytes 57349 | tf_op jit(solution)/shard_map/while/body/eval_jaxpr/in,ic->cn/dot_general | solution.py:147
  55.5 3.1 %broadcast_multiply_fusion.4 = f32[2048,128,4]{0,2,1:T(4,128)} fusion(f32[2048,4]{0,1:T(4,128)S(1)} %get-tuple-element.550, f32[2048,128]{0,1:T(8,128)S(1)} %get-tuple-element.563), kind=kLoop, calls=%fused_computation.35.clone.1 | loop fusion | flops 1048576 | bytes 5275648 | tf_op jit(solution)/shard_map/while/body/eval_jaxpr/mul | solution.py:137
  58.6 3.2 %broadcast_multiply_fusion.5 = f32[2048,128,4]{0,2,1:T(4,128)} fusion(f32[2048,4]{0,1:T(4,128)S(1)} %get-tuple-element.564, f32[2048,128]{0,1:T(8,128)S(1)} %get-tuple-element.565), kind=kLoop, calls=%fused_computation.36.clone.1 | loop fusion | flops 1048576 | bytes 5275648 | tf_op jit(solution)/shard_map/while/body/eval_jaxpr/mul | solution.py:136
  61.8 9.3 %fusion.136 = f32[128,1024]{1,0:T(8,128)S(1)} fusion(f32[2048,128,4]{0,2,1:T(4,128)} %broadcast_multiply_fusion.4, f32[2048,128,4]{0,2,1:T(4,128)} %broadcast_multiply_fusion.5, f32[128,1024]{1,0:T(8,128)S(1)} %get-tuple-element.580, s32[2048]{0:T(1024)S(1)} %bitcast.454, pred[]{:T(512)S(6)} %compare.4), kind=kOutput, calls=%fused_computation.37.clone.1 | convolution fusion | flops 3224109056 | bytes 9445377 | tf_op jit(solution)/shard_map/while/body/eval_jaxpr/ib,im->bm/dot_general | solution.py:143
  71.1 5.4 %fusion.137 = f32[2,2048]{1,0:T(2,128)S(1)} fusion(s32[2048]{0:T(1024)S(1)} %bitcast.470, f32[2,2048]{1,0:T(2,128)S(1)} %get-tuple-element.581, f32[4,2048,2]{1,2,0:T(2,128)S(1)} %get-tuple-element.599, s32[]{:T(128)S(6)} %copy.66, pred[]{:T(512)S(6)} %compare.4), kind=kOutput, calls=%fused_computation.34.clone.1 | convolution fusion | flops 104865792 | bytes 57349 | tf_op jit(solution)/shard_map/while/body/eval_jaxpr/in,ic->cn/dot_general | solution.py:147
  77.2 3.1 %broadcast_multiply_fusion.4 = f32[2048,128,4]{0,2,1:T(4,128)} fusion(f32[2048,4]{0,1:T(4,128)S(1)} %get-tuple-element.550, f32[2048,128]{0,1:T(8,128)S(1)} %get-tuple-element.563), kind=kLoop, calls=%fused_computation.35.clone.1 | loop fusion | flops 1048576 | bytes 5275648 | tf_op jit(solution)/shard_map/while/body/eval_jaxpr/mul | solution.py:137
  80.4 3.2 %broadcast_multiply_fusion.5 = f32[2048,128,4]{0,2,1:T(4,128)} fusion(f32[2048,4]{0,1:T(4,128)S(1)} %get-tuple-element.564, f32[2048,128]{0,1:T(8,128)S(1)} %get-tuple-element.565), kind=kLoop, calls=%fused_computation.36.clone.1 | loop fusion | flops 1048576 | bytes 5275648 | tf_op jit(solution)/shard_map/while/body/eval_jaxpr/mul | solution.py:136
  83.5 9.3 %fusion.136 = f32[128,1024]{1,0:T(8,128)S(1)} fusion(f32[2048,128,4]{0,2,1:T(4,128)} %broadcast_multiply_fusion.4, f32[2048,128,4]{0,2,1:T(4,128)} %broadcast_multiply_fusion.5, f32[128,1024]{1,0:T(8,128)S(1)} %get-tuple-element.580, s32[2048]{0:T(1024)S(1)} %bitcast.454, pred[]{:T(512)S(6)} %compare.4), kind=kOutput, calls=%fused_computation.37.clone.1 | convolution fusion | flops 3224109056 | bytes 9445377 | tf_op jit(solution)/shard_map/while/body/eval_jaxpr/ib,im->bm/dot_general | solution.py:143
  92.8 5.4 %fusion.137 = f32[2,2048]{1,0:T(2,128)S(1)} fusion(s32[2048]{0:T(1024)S(1)} %bitcast.470, f32[2,2048]{1,0:T(2,128)S(1)} %get-tuple-element.581, f32[4,2048,2]{1,2,0:T(2,128)S(1)} %get-tuple-element.599, s32[]{:T(128)S(6)} %copy.66, pred[]{:T(512)S(6)} %compare.4), kind=kOutput, calls=%fused_computation.34.clone.1 | convolution fusion | flops 104865792 | bytes 57349 | tf_op jit(solution)/shard_map/while/body/eval_jaxpr/in,ic->cn/dot_general | solution.py:147
  98.3 0.9 reshape.3148
  99.3 7.3 %all-to-all-start = ((f32[32,4,1024]{2,1,0:T(4,128)}), f32[32,4,1024]{2,1,0:T(4,128)S(1)}, u32[]{:S(2)}, u32[]{:S(2)}) async-start(f32[32,4,1024]{2,1,0:T(4,128)} %reshape.3148), calls=%async_computation | async-start | bytes 1048576 | tf_op jit(solution)/shard_map/all_to_all | solution.py:164
  106.9 0.6 stack.118
  107.6 40.8 %psum.7 = f32[2,2048]{1,0:T(2,128)S(1)} all-reduce(f32[2,2048]{1,0:T(2,128)S(1)} %get-tuple-element.135), channel_id=1, replica_groups=mesh['src'=8,'att'=4] {'src','att'}, use_global_device_ids=true, to_apply=%region_3.4 | all-reduce | flops 4096 | bytes 32768 | tf_op jit(solution)/shard_map/psum | solution.py:165
  149.7 0.9 copy.46
  150.5 4.4 %all-to-all-start.1 = ((f32[32,4,512]{2,1,0:T(4,128)}), f32[32,4,512]{2,1,0:T(4,128)S(1)}, u32[]{:S(2)}, u32[]{:S(2)}) async-start(f32[32,4,512]{2,1,0:T(4,128)} %copy.46), calls=%async_computation.1 | async-start | bytes 524288 | tf_op jit(solution)/shard_map/all_to_all | solution.py:185
  155.6 9.9 %all-to-all-done.1 = f32[32,4,512]{2,1,0:T(4,128)S(1)} async-done(((f32[32,4,512]{2,1,0:T(4,128)}), f32[32,4,512]{2,1,0:T(4,128)S(1)}, u32[]{:S(2)}, u32[]{:S(2)}) %all-to-all-start.1) | async-done | bytes 262176 | tf_op jit(solution)/shard_map/all_to_all | solution.py:185
  165.7 90.2 %while.24 = (s32[]{:T(128)}, f32[4,2048]{1,0:T(4,128)S(1)}, f32[4,2048]{1,0:T(4,128)S(1)}, s32[4,2048]{1,0:T(4,128)S(1)}, f32[4,2048,4]{1,2,0:T(4,128)S(1)}, /*i...) while((s32[]{:T(128)}, f32[4,2048]{1,0:T(4,128)S(1)}, ...), condition=%wide.region_7.8_spmd.clone, body=%wide.region_4.7_spmd.clone.sunk | while | flops 1670653952 | bytes 19644568 | solution.py:215
  165.7 7.5 %fusion.130 = f32[1,2048]{1,0:T(1,128)S(1)} fusion(f32[2048,1]{0,1:T(1,128)S(1)} %bitcast.504, s32[2048]{0:T(1024)S(1)} %bitcast.471), kind=kOutput, calls=%fused_computation.5.clone.1 | convolution fusion | flops 54525952 | bytes 24576 | tf_op jit(solution)/shard_map/while/body/eval_jaxpr/dot_general | solution.py:201
  173.3 3.7 %fusion.131 = f32[2048,512]{0,1:T(8,128)} fusion(f32[128,512]{1,0:T(8,128)S(1)} %get-tuple-element.635, s32[2048]{0:T(1024)S(1)} %bitcast.446), kind=kOutput, calls=%fused_computation.14.clone.1 | convolution fusion | flops 1610874880 | bytes 4464640 | tf_op jit(solution)/shard_map/while/body/eval_jaxpr/dot_general | solution.py:193
  177.0 5.2 %reshape.3266 = f32[2048,128,4]{0,2,1:T(4,128)} reshape(f32[2048,512]{0,1:T(8,128)} %fusion.131) | data formatting | bytes 8388608 | tf_op jit(solution)/shard_map/while/body/eval_jaxpr/reshape | solution.py:196
  182.2 5.3 %multiply_reduce_fusion.5 = f32[2048,128]{0,1:T(8,128)S(1)} fusion(f32[2048,128,4]{0,2,1:T(4,128)} %reshape.3266, f32[2048,4]{0,1:T(4,128)S(1)} %get-tuple-element.531), kind=kLoop, calls=%fused_computation.7.clone.1 | loop fusion | flops 1835008 | bytes 5275648 | tf_op jit(solution)/shard_map/while/body/eval_jaxpr/reduce_sum | solution.py:197
  188.3 7.5 %fusion.130 = f32[1,2048]{1,0:T(1,128)S(1)} fusion(f32[2048,1]{0,1:T(1,128)S(1)} %bitcast.504, s32[2048]{0:T(1024)S(1)} %bitcast.471), kind=kOutput, calls=%fused_computation.5.clone.1 | convolution fusion | flops 54525952 | bytes 24576 | tf_op jit(solution)/shard_map/while/body/eval_jaxpr/dot_general | solution.py:201
  195.8 3.7 %fusion.131 = f32[2048,512]{0,1:T(8,128)} fusion(f32[128,512]{1,0:T(8,128)S(1)} %get-tuple-element.635, s32[2048]{0:T(1024)S(1)} %bitcast.446), kind=kOutput, calls=%fused_computation.14.clone.1 | convolution fusion | flops 1610874880 | bytes 4464640 | tf_op jit(solution)/shard_map/while/body/eval_jaxpr/dot_general | solution.py:193
  199.6 5.2 %reshape.3266 = f32[2048,128,4]{0,2,1:T(4,128)} reshape(f32[2048,512]{0,1:T(8,128)} %fusion.131) | data formatting | bytes 8388608 | tf_op jit(solution)/shard_map/while/body/eval_jaxpr/reshape | solution.py:196
  204.7 5.3 %multiply_reduce_fusion.5 = f32[2048,128]{0,1:T(8,128)S(1)} fusion(f32[2048,128,4]{0,2,1:T(4,128)} %reshape.3266, f32[2048,4]{0,1:T(4,128)S(1)} %get-tuple-element.531), kind=kLoop, calls=%fused_computation.7.clone.1 | loop fusion | flops 1835008 | bytes 5275648 | tf_op jit(solution)/shard_map/while/body/eval_jaxpr/reduce_sum | solution.py:197
  210.8 7.5 %fusion.130 = f32[1,2048]{1,0:T(1,128)S(1)} fusion(f32[2048,1]{0,1:T(1,128)S(1)} %bitcast.504, s32[2048]{0:T(1024)S(1)} %bitcast.471), kind=kOutput, calls=%fused_computation.5.clone.1 | convolution fusion | flops 54525952 | bytes 24576 | tf_op jit(solution)/shard_map/while/body/eval_jaxpr/dot_general | solution.py:201
  218.3 3.7 %fusion.131 = f32[2048,512]{0,1:T(8,128)} fusion(f32[128,512]{1,0:T(8,128)S(1)} %get-tuple-element.635, s32[2048]{0:T(1024)S(1)} %bitcast.446), kind=kOutput, calls=%fused_computation.14.clone.1 | convolution fusion | flops 1610874880 | bytes 4464640 | tf_op jit(solution)/shard_map/while/body/eval_jaxpr/dot_general | solution.py:193
  222.1 5.2 %reshape.3266 = f32[2048,128,4]{0,2,1:T(4,128)} reshape(f32[2048,512]{0,1:T(8,128)} %fusion.131) | data formatting | bytes 8388608 | tf_op jit(solution)/shard_map/while/body/eval_jaxpr/reshape | solution.py:196
  227.3 5.3 %multiply_reduce_fusion.5 = f32[2048,128]{0,1:T(8,128)S(1)} fusion(f32[2048,128,4]{0,2,1:T(4,128)} %reshape.3266, f32[2048,4]{0,1:T(4,128)S(1)} %get-tuple-element.531), kind=kLoop, calls=%fused_computation.7.clone.1 | loop fusion | flops 1835008 | bytes 5275648 | tf_op jit(solution)/shard_map/while/body/eval_jaxpr/reduce_sum | solution.py:197
  233.4 7.5 %fusion.130 = f32[1,2048]{1,0:T(1,128)S(1)} fusion(f32[2048,1]{0,1:T(1,128)S(1)} %bitcast.504, s32[2048]{0:T(1024)S(1)} %bitcast.471), kind=kOutput, calls=%fused_computation.5.clone.1 | convolution fusion | flops 54525952 | bytes 24576 | tf_op jit(solution)/shard_map/while/body/eval_jaxpr/dot_general | solution.py:201
  240.9 3.7 %fusion.131 = f32[2048,512]{0,1:T(8,128)} fusion(f32[128,512]{1,0:T(8,128)S(1)} %get-tuple-element.635, s32[2048]{0:T(1024)S(1)} %bitcast.446), kind=kOutput, calls=%fused_computation.14.clone.1 | convolution fusion | flops 1610874880 | bytes 4464640 | tf_op jit(solution)/shard_map/while/body/eval_jaxpr/dot_general | solution.py:193
  244.6 5.2 %reshape.3266 = f32[2048,128,4]{0,2,1:T(4,128)} reshape(f32[2048,512]{0,1:T(8,128)} %fusion.131) | data formatting | bytes 8388608 | tf_op jit(solution)/shard_map/while/body/eval_jaxpr/reshape | solution.py:196
  249.8 5.3 %multiply_reduce_fusion.5 = f32[2048,128]{0,1:T(8,128)S(1)} fusion(f32[2048,128,4]{0,2,1:T(4,128)} %reshape.3266, f32[2048,4]{0,1:T(4,128)S(1)} %get-tuple-element.531), kind=kLoop, calls=%fused_computation.7.clone.1 | loop fusion | flops 1835008 | bytes 5275648 | tf_op jit(solution)/shard_map/while/body/eval_jaxpr/reduce_sum | solution.py:197
  (154 shorter events, 11.6 us)
Async XLA Ops:
  0.6 0.7 copy-start
  0.6 10.0 %copy-start.1 = (f32[5,8192]{1,0:T(8,128)S(1)}, f32[5,8192]{1,0:T(8,128)}, u32[]{:S(2)}) copy-start(f32[5,8192]{1,0:T(8,128)} %param.19) | copy-start | bytes 491524
  0.7 10.1 %copy-start.3 = (f32[8192]{0:T(1024)S(1)}, f32[8192]{0:T(1024)}, u32[]{:S(2)}) copy-start(f32[8192]{0:T(1024)} %param.21) | copy-start | bytes 98308
  0.7 10.1 %copy-start.4 = (f32[8192]{0:T(1024)S(1)}, f32[8192]{0:T(1024)}, u32[]{:S(2)}) copy-start(f32[8192]{0:T(1024)} %param.17) | copy-start | bytes 98308
  0.7 7.3 %copy-start.5 = (s32[8192]{0:T(1024)S(1)}, s32[8192]{0:T(1024)}, u32[]{:S(2)}) copy-start(s32[8192]{0:T(1024)} %param.25) | copy-start | bytes 98308
  0.7 7.3 %copy-start.6 = (s32[8192]{0:T(1024)S(1)}, s32[8192]{0:T(1024)}, u32[]{:S(2)}) copy-start(s32[8192]{0:T(1024)} %param.24) | copy-start | bytes 98308
  0.7 7.4 %copy-start.8 = (s32[8192]{0:T(1024)S(1)}, s32[8192]{0:T(1024)}, u32[]{:S(2)}) copy-start(s32[8192]{0:T(1024)} %param.26) | copy-start | bytes 98308
  0.7 7.4 %copy-start.7 = (f32[8192]{0:T(1024)S(1)}, f32[8192]{0:T(1024)}, u32[]{:S(2)}) copy-start(f32[8192]{0:T(1024)} %param.22) | copy-start | bytes 98308
  0.7 10.1 %copy-start.9 = (s32[8192]{0:T(1024)S(1)}, s32[8192]{0:T(1024)}, u32[]{:S(2)}) copy-start(s32[8192]{0:T(1024)} %param.27) | copy-start | bytes 98308
  0.7 10.1 %copy-start.2 = (f32[4,8192]{1,0:T(4,128)S(1)}, f32[4,8192]{1,0:T(4,128)}, u32[]{:S(2)}) copy-start(f32[4,8192]{1,0:T(4,128)} %param.20) | copy-start | bytes 393220
  11.1 95.5 %copy-start.10 = (s32[32,1,4]{0,2,1:T(4,128)S(1)}, s32[32,1,4]{0,2,1:T(4,128)}, u32[]{:S(2)}) copy-start(s32[32,1,4]{0,2,1:T(4,128)} %param.29) | copy-start | bytes 1540
  99.3 49.1 %all-to-all-start = ((f32[32,4,1024]{2,1,0:T(4,128)}), f32[32,4,1024]{2,1,0:T(4,128)S(1)}, u32[]{:S(2)}, u32[]{:S(2)}) async-start(f32[32,4,1024]{2,1,0:T(4,128)} %reshape.3148), calls=%async_computation | async-start | bytes 1048576 | tf_op jit(solution)/shard_map/all_to_all | solution.py:164
  150.5 15.0 %all-to-all-start.1 = ((f32[32,4,512]{2,1,0:T(4,128)}), f32[32,4,512]{2,1,0:T(4,128)S(1)}, u32[]{:S(2)}, u32[]{:S(2)}) async-start(f32[32,4,512]{2,1,0:T(4,128)} %copy.46), calls=%async_computation.1 | async-start | bytes 524288 | tf_op jit(solution)/shard_map/all_to_all | solution.py:185
  255.9 0.6 copy-start.11
where the time goes:
time: 258 us; the launch traced here: 256 us
  matrix products  106 us (41%)
  other arithmetic  53.4 us (21%)
  blocking collectives  40.8 us (16%)
  local copies, waits for them, and re-layouts  32.3 us (13%)
  starting transfers between devices  11.7 us (5%)
  waiting for transfers between devices  9.94 us (4%)
    psum x1, blocking collectives, on_device(): totals = lax.psum(calib_terms, ('src', 'att'))  40.8 us
    dot_general x4, matrix products, accumulate(): jnp.einsum('ib,im->bm', selector, spread, precision=HIGH, preferred_eleme...  37.2 us
    dot_general x4, matrix products, correct(): jnp.dot(calib_hot, calib_update, precision=HIGH, preferred_element_type=j...  30.1 us
    dot_general x4, matrix products, accumulate(): jnp.einsum('in,ic->cn', calib_hot, calib_vals, precision=HIGH, preferred_...  21.4 us
    reduce_sum x4, other arithmetic, correct(): projected = jnp.sum(fetched * attitude_block[:, None, :], axis=2)  21.3 us
    reshape x4, local copies, waits for them, and re-layouts, correct(): fetched = fetched.reshape(step_rows, KNOT, 4)  20.7 us
    dot_general x4, matrix products, correct(): jnp.dot(selector_rows, segment_rows, precision=HIGH, preferred_element_ty...  15 us
    mul x4, other arithmetic, accumulate(): linear[:, :, None] * rhs_part[:, None, :]  12.7 us
  transfers between devices with their start and end apart: 2, of which 1 were waited for; matrix products, arithmetic and copies ran while one was open for 1% of the time, Pallas kernels for 0%

commit v1 on v0

v1 whole, which is shorter than its diff:
```python
import functools

import jax
import jax.numpy as jnp
from jax import lax
from jax.experimental import pallas as pl
from jax.experimental.pallas import tpu as pltpu
from jax.sharding import PartitionSpec as P

OBS_TILE = 2048
SRC_TILE = 64
KNOT = 128
LIST = 4
KB_DEV = 8
NCAL = 2048

HALF = 64
WIN = 72
LO = 64
CHUNK = 1024
F32 = jnp.float32
BF16 = jnp.bfloat16
NT = (((1,), (1,)), ((), ()))
NN = (((1,), (0,)), ((), ()))


def mm(left, right, dims):
    return lax.dot_general(left, right, dims, preferred_element_type=F32)


def split2(value):
    high = value.astype(BF16)
    low = (value - high.astype(F32)).astype(BF16)
    return high, low


def split3(value):
    high = value.astype(BF16)
    rest = value - high.astype(F32)
    middle = rest.astype(BF16)
    low = (rest - middle.astype(F32)).astype(BF16)
    return high, middle, low


def hot(rows, index):
    count = index.shape[1]
    match = lax.broadcasted_iota(jnp.int32, (rows, count), 0) == index
    return jnp.where(match, F32(1.0), F32(0.0)).astype(BF16)


def kernel(
    devices,
    n_att,
    count_ref,
    residual,
    weight,
    source_part,
    attitude_part,
    calib_part,
    phase,
    obs_source,
    obs_owner,
    obs_slot,
    obs_knot,
    obs_calib,
    list_row,
    list_col,
    source_out,
    attitude_out,
    calib_out,
    residual_out,
    sel,
    lin_all,
    first_all,
    weighted_all,
    calhot,
    srchot,
    acc,
    acc_cal,
    cdiag_keep,
    send_diag,
    send_rhs,
    recv_diag,
    recv_rhs,
    send_ret,
    recv_ret,
    send_cal,
    recv_cal,
    send_calret,
    recv_calret,
    send_sem,
    recv_sem,
):
    rows_a = devices * LIST * 2
    count = residual.shape[1]
    tiles = count // OBS_TILE
    share = NCAL // devices
    me_src = lax.axis_index("src")
    me_att = lax.axis_index("att")
    me = me_src * n_att + me_att

    def peer_of(step):
        peer = lax.rem(me + step, devices)
        return peer, (peer // n_att, lax.rem(peer, n_att))

    barrier = pltpu.get_barrier_semaphore()

    def greet(step, carry):
        _, where = peer_of(step)
        pl.semaphore_signal(
            barrier, inc=1, device_id=where, device_id_type=pl.DeviceIdType.MESH
        )
        return carry

    lax.fori_loop(1, devices, greet, 0)

    def spread(source, target, which):
        def one(step, carry):
            peer, where = peer_of(step)
            pltpu.make_async_remote_copy(
                src_ref=source.at[peer],
                dst_ref=target.at[me],
                send_sem=send_sem.at[which],
                recv_sem=recv_sem.at[which],
                device_id=where,
                device_id_type=pl.DeviceIdType.MESH,
            ).start()
            return carry

        pltpu.make_async_copy(source.at[me], target.at[me], recv_sem.at[which]).start()
        lax.fori_loop(1, devices, one, 0)

    def arrive(target, which):
        pltpu.make_async_copy(target, target, recv_sem.at[which]).wait()

    def left(source, which):
        part = source.at[pl.ds(0, devices - 1)]
        pltpu.make_async_copy(part, part, send_sem.at[which]).wait()

    def packed(sums):
        odd = lax.rem(lax.broadcasted_iota(jnp.int32, (8, rows_a), 1), 2) == 1
        pieces = []
        for c in range(4):
            block = sums[c * WIN : (c + 1) * WIN]
            over = pltpu.roll(block[HALF:WIN], 1, 1)
            pieces.append(block[0:8] + jnp.where(odd, over, F32(0.0)))
            pieces.append(block[8:HALF])
        return jnp.concatenate(pieces, 0).T

    acc[...] = jnp.zeros_like(acc)
    acc_cal[...] = jnp.zeros_like(acc_cal)
    per_tile = OBS_TILE // CHUNK

    def diag_step(step, carry):
        here = pl.ds(pl.multiple_of(step * CHUNK, CHUNK), CHUNK)
        tile = step // per_tile
        place = lax.broadcasted_iota(jnp.int32, (1, CHUNK), 1) + (step - tile * per_tile) * CHUNK
        weighted = jnp.where(place < count_ref[0, tile], weight[:, here], F32(0.0))
        weighted_all[:, here] = weighted
        u = phase[:, here]
        other = 1.0 - u
        square = u * u
        cube = square * u
        b0 = other * other * other / 6.0
        b1 = (3.0 * cube - 6.0 * square + 4.0) / 6.0
        b2 = (-3.0 * cube + 3.0 * square + 3.0 * u + 1.0) / 6.0
        b3 = cube / 6.0
        knot = obs_knot[:, here]
        half = knot // HALF
        row = (obs_owner[:, here] * LIST + obs_slot[:, here]) * 2 + half
        chosen = hot(rows_a, row)
        sel[:, here] = chosen
        away = lax.broadcasted_iota(jnp.int32, (WIN, CHUNK), 0) - (knot - half * HALF)
        lin = jnp.where(
            away == 0,
            b0,
            jnp.where(
                away == 1, b1, jnp.where(away == 2, b2, jnp.where(away == 3, b3, F32(0.0)))
            ),
        )
        lin_all[:, here] = lin
        squares = lin * lin
        att = attitude_part[:, here]
        value = jnp.concatenate(
            [squares * (weighted * att[c : c + 1] * att[c : c + 1]) for c in range(4)], 0
        )
        high, low = split2(value)
        acc[...] += mm(high, chosen, NT) + mm(low, chosen, NT)
        unit = obs_calib[:, here]
        group = unit // share
        calibs = hot(LO, unit - group * share)
        calhot[:, here] = calibs
        part = calib_part[:, here]
        match = lax.broadcasted_iota(jnp.int32, (devices, CHUNK), 0) == group
        chigh, clow = split2(jnp.where(match, weighted * part * part, F32(0.0)))
        acc_cal[...] += mm(chigh, calibs, NT) + mm(clow, calibs, NT)
        return carry

    lax.fori_loop(0, count // CHUNK, diag_step, 0)
    send_diag[...] = packed(acc[...]).reshape(devices, 8, 4 * HALF)
    cdiag_keep[...] = acc_cal[...]

    pl.semaphore_wait(barrier, devices - 1)
    spread(send_diag, recv_diag, 0)

    all_sums = []
    for tile in range(tiles):
        here = pl.ds(tile * OBS_TILE, OBS_TILE)
        res = residual[:, here]
        parts = source_part[:, here]
        block = jnp.concatenate([parts, res, jnp.zeros((2, OBS_TILE), F32)], 0)
        weighted = weighted_all[:, here]
        columns = jnp.concatenate(
            [block * (weighted * parts[k : k + 1]) for k in range(5)]
            + [jnp.zeros((8, OBS_TILE), F32)],
            0,
        )
        stars = hot(SRC_TILE, obs_source[:, here])
        srchot[:, here] = stars
        high, middle, low = split3(columns)
        all_sums.append(mm(high, stars, NT) + (mm(middle, stars, NT) + mm(low, stars, NT)))
    sums = jnp.concatenate(all_sums, 1)
    matrix = [[sums[8 * min(l, r) + max(l, r)][None, :] for r in range(5)] for l in range(5)]
    target = [sums[8 * l + 5][None, :] for l in range(5)]
    for l in range(5):
        matrix[l][l] = matrix[l][l] + 1.0
    for pivot in range(5):
        for lower in range(pivot + 1, 5):
            factor = matrix[lower][pivot] / matrix[pivot][pivot]
            for r in range(pivot, 5):
                matrix[lower][r] = matrix[lower][r] - factor * matrix[pivot][r]
            target[lower] = target[lower] - factor * target[pivot]
    result = [None] * 5
    for pivot in range(4, -1, -1):
        value = target[pivot]
        for r in range(pivot + 1, 5):
            value = value - matrix[pivot][r] * result[r]
        result[pivot] = value / matrix[pivot][pivot]
    update = jnp.concatenate(result, 0)
    source_out[...] = update
    update8 = jnp.concatenate(result + [jnp.zeros((3, tiles * SRC_TILE), F32)], 0)
    uhigh, umiddle, ulow = split3(jnp.concatenate([update8, jnp.zeros_like(update8)], 0))
    for tile in range(tiles):
        here = pl.ds(tile * OBS_TILE, OBS_TILE)
        mine = slice(tile * SRC_TILE, (tile + 1) * SRC_TILE)
        stars = srchot[:, here]
        per_obs = mm(uhigh[:, mine], stars, NN) + (
            mm(umiddle[:, mine], stars, NN) + mm(ulow[:, mine], stars, NN)
        )
        first_all[:, here] = residual[:, here] - jnp.sum(
            source_part[:, here] * per_obs[0:5], axis=0, keepdims=True
        )

    acc[...] = jnp.zeros_like(acc)
    acc_cal[...] = jnp.zeros_like(acc_cal)

    def rhs_step(step, carry):
        here = pl.ds(pl.multiple_of(step * CHUNK, CHUNK), CHUNK)
        lin = lin_all[:, here]
        chosen = sel[:, here]
        scaled = weighted_all[:, here] * first_all[:, here]
        att = attitude_part[:, here]
        value = jnp.concatenate([lin * (scaled * att[c : c + 1]) for c in range(4)], 0)
        high, low = split2(value)
        acc[...] += mm(high, chosen, NT) + mm(low, chosen, NT)
        group = obs_calib[:, here] // share
        match = lax.broadcasted_iota(jnp.int32, (devices, CHUNK), 0) == group
        chigh, clow = split2(jnp.where(match, scaled * calib_part[:, here], F32(0.0)))
        calibs = calhot[:, here]
        acc_cal[...] += mm(chigh, calibs, NT) + mm(clow, calibs, NT)
        return carry

    lax.fori_loop(0, count // CHUNK, rhs_step, 0)
    send_rhs[...] = packed(acc[...]).reshape(devices, 8, 4 * HALF)
    spread(send_rhs, recv_rhs, 1)
    both = jnp.concatenate([acc_cal[...], cdiag_keep[...]], 1)
    send_cal[...] = both[:, None, :]
    spread(send_cal, recv_cal, 2)

    blocks = KB_DEV * 2
    wide = lax.broadcasted_iota(jnp.int32, (blocks, rows_a), 0)
    wide_half = lax.rem(lax.broadcasted_iota(jnp.int32, (blocks, rows_a), 1), 2)
    gather = jnp.where(wide == wide_half * KB_DEV + list_row[...], F32(1.0), F32(0.0)).astype(BF16)
    tall = lax.broadcasted_iota(jnp.int32, (rows_a, blocks), 1)
    tall_half = lax.rem(lax.broadcasted_iota(jnp.int32, (rows_a, blocks), 0), 2)
    scatter = jnp.where(tall == tall_half * KB_DEV + list_col[...], F32(1.0), F32(0.0)).astype(BF16)

    def owned(arrived):
        high, middle, low = split3(arrived[...].reshape(rows_a, 4 * HALF))
        return mm(gather, high, NN) + (mm(gather, middle, NN) + mm(gather, low, NN))

    arrive(recv_diag, 0)
    diag = owned(recv_diag)
    arrive(recv_rhs, 1)
    coef = owned(recv_rhs) / (diag + 1.0)
    high, middle, low = split3(coef)
    back = mm(scatter, high, NN) + (mm(scatter, middle, NN) + mm(scatter, low, NN))
    send_ret[...] = back.reshape(devices, 8, 4 * HALF)
    spread(send_ret, recv_ret, 3)
    arrive(recv_cal, 2)
    calsum = jnp.sum(recv_cal[...], axis=0)
    ratio = calsum / (pltpu.roll(calsum, LO, 1) + 1.0)
    send_calret[...] = ratio

    def one_cal(step, carry):
        _, where = peer_of(step)
        pltpu.make_async_remote_copy(
            src_ref=send_calret,
            dst_ref=recv_calret.at[me],
            send_sem=send_sem.at[4],
            recv_sem=recv_sem.at[4],
            device_id=where,
            device_id_type=pl.DeviceIdType.MESH,
        ).start()
        return carry

    pltpu.make_async_copy(send_calret, recv_calret.at[me], recv_sem.at[4]).start()
    lax.fori_loop(1, devices, one_cal, 0)
    for c in range(4):
        wide_rows = jnp.concatenate(
            [
                coef[0:KB_DEV, c * HALF : (c + 1) * HALF],
                coef[KB_DEV:blocks, c * HALF : (c + 1) * HALF],
            ],
            1,
        )
        for block in range(KB_DEV):
            attitude_out[c : c + 1, block * KNOT : (block + 1) * KNOT] = wide_rows[
                block : block + 1
            ]

    arrive(recv_calret, 4)
    calvals = recv_calret[...]
    calib_out[...] = calvals
    ctable = jnp.concatenate(split2(calvals.reshape(devices, 2 * LO)[:, 0:LO]), 0)
    arrive(recv_ret, 3)
    table = recv_ret[...].reshape(rows_a, 4 * HALF).T
    even = lax.rem(lax.broadcasted_iota(jnp.int32, (8, rows_a), 1), 2) == 0
    pieces = []
    for c in range(4):
        own = table[c * HALF : (c + 1) * HALF]
        pieces.append(own)
        pieces.append(jnp.where(even, pltpu.roll(own[0:8], rows_a - 1, 1), F32(0.0)))
    tables = jnp.concatenate(split2(jnp.concatenate(pieces, 0)), 0)
    acc_shape = 4 * WIN

    def correct_step(step, carry):
        here = pl.ds(pl.multiple_of(step * CHUNK, CHUNK), CHUNK)
        fetched = mm(tables, sel[:, here], NN)
        fetched = fetched[0:acc_shape] + fetched[acc_shape : 2 * acc_shape]
        att = attitude_part[:, here]
        projected = fetched[0:WIN] * att[0:1]
        for c in range(1, 4):
            projected = projected + fetched[c * WIN : (c + 1) * WIN] * att[c : c + 1]
        term = jnp.sum(projected * lin_all[:, here], axis=0, keepdims=True)
        group = obs_calib[:, here] // share
        match = lax.broadcasted_iota(jnp.int32, (devices, CHUNK), 0) == group
        cal = mm(ctable, calhot[:, here], NN)
        cal = jnp.where(match, cal[0:devices] + cal[devices : 2 * devices], F32(0.0))
        value = jnp.sum(cal, axis=0, keepdims=True)
        residual_out[:, here] = first_all[:, here] - term - calib_part[:, here] * value
        return carry

    lax.fori_loop(0, count // CHUNK, correct_step, 0)
    left(send_diag, 0)
    left(send_rhs, 1)
    left(send_cal, 2)
    left(send_ret, 3)
    part = recv_calret.at[pl.ds(0, devices - 1)]
    pltpu.make_async_copy(part, part, send_sem.at[4]).wait()


def on_device(n_src, n_att, *args):
    (
        residual,
        weight,
        source_part,
        attitude_part,
        calib_part,
        phase,
        obs_source,
        obs_owner,
        obs_slot,
        obs_knot,
        obs_calib,
        tile_count,
        time_list,
    ) = args
    devices = n_src * n_att
    count = residual.shape[0]
    sources = count // OBS_TILE * SRC_TILE
    rows_a = devices * LIST * 2
    listed = jnp.repeat(time_list.reshape(devices * LIST), 2)
    row = lambda x: x.reshape(1, count)
    vmem = pl.BlockSpec(memory_space=pltpu.VMEM)
    slab = pltpu.VMEM((devices, 8, 4 * HALF), F32)
    line = pltpu.VMEM((devices, 1, 2 * LO), F32)
    source_update, attitude_update, calib, residual_out = pl.pallas_call(
        functools.partial(kernel, devices, n_att),
        out_shape=(
            jax.ShapeDtypeStruct((5, sources), F32),
            jax.ShapeDtypeStruct((4, KB_DEV * KNOT), F32),
            jax.ShapeDtypeStruct((devices, 1, 2 * LO), F32),
            jax.ShapeDtypeStruct((1, count), F32),
        ),
        in_specs=[pl.BlockSpec(memory_space=pltpu.SMEM)] + [vmem] * 13,
        out_specs=(vmem,) * 4,
        scratch_shapes=[
            pltpu.VMEM((rows_a, count), BF16),
            pltpu.VMEM((WIN, count), F32),
            pltpu.VMEM((1, count), F32),
            pltpu.VMEM((1, count), F32),
            pltpu.VMEM((LO, count), BF16),
            pltpu.VMEM((SRC_TILE, count), BF16),
            pltpu.VMEM((4 * WIN, rows_a), F32),
            pltpu.VMEM((devices, LO), F32),
            pltpu.VMEM((devices, LO), F32),
            slab,
            slab,
            slab,
            slab,
            slab,
            slab,
            line,
            line,
            pltpu.VMEM((1, 2 * LO), F32),
            line,
            pltpu.SemaphoreType.DMA((5,)),
            pltpu.SemaphoreType.DMA((5,)),
        ],
        compiler_params=pltpu.CompilerParams(
            collective_id=0, has_side_effects=True, vmem_limit_bytes=56 * 1024 * 1024
        ),
    )(
        tile_count,
        row(residual),
        row(weight),
        source_part,
        attitude_part,
        row(calib_part),
        row(phase),
        row(obs_source),
        row(obs_owner),
        row(obs_slot),
        row(obs_knot),
        row(obs_calib),
        listed.reshape(1, rows_a),
        listed.reshape(rows_a, 1),
    )
    calib_update = calib[:, 0, 0 : NCAL // devices].reshape(NCAL)
    return source_update, attitude_update, calib_update, residual_out.reshape(count)


def solution(mesh):
    both = P(("src", "att"))
    columns = P(None, ("src", "att"))
    placed = (
        both,
        both,
        columns,
        columns,
        both,
        both,
        both,
        both,
        both,
        both,
        both,
        P(("src", "att"), None),
        P(None, ("src", "att"), None),
    )
    return jax.shard_map(
        functools.partial(on_device, mesh.shape["src"], mesh.shape["att"]),
        mesh=mesh,
        in_specs=placed,
        out_specs=(columns, columns, P(), both),
        check_vma=False,
    )
```

time: 258 us -> 47.9 us (0.19)
  matrix products: 106 us -> 0 us
  other arithmetic: 53.4 us -> 0 us
  Pallas kernels: 0 us -> 41.3 us
  blocking collectives: 40.8 us -> 0 us
  local copies, waits for them, and re-layouts: 32.3 us -> 5.67 us
  starting transfers between devices: 11.7 us -> 0 us
  waiting for transfers between devices: 9.94 us -> 0 us
    dot_general x20 -> x0, matrix products: 106 us -> none  [the longest x4 37.2 us: accumulate(): jnp.einsum('ib,im->bm', selector, spread, precision=HIGH, preferred_eleme...]
    pallas_call x0 -> x1, Pallas kernels: none -> 41.3 us  [on_device(): pl.pallas_call(functools.partial(kernel, devices, n_att), out_shape=(jax....]
    psum x1 -> x0, blocking collectives: 40.8 us -> none  [on_device(): totals = lax.psum(calib_terms, ('src', 'att'))]
    mul x13 -> x0, other arithmetic: 26.9 us -> none  [the longest x4 12.7 us: accumulate(): linear[:, :, None] * rhs_part[:, None, :]]
    reduce_sum x9 -> x0, other arithmetic: 23.3 us -> none  [the longest x4 21.3 us: correct(): projected = jnp.sum(fetched * attitude_block[:, None, :], axis=2)]
    reshape x13 -> x1, local copies, waits for them, and re-layouts: 22 us -> 0.1 us  [on_device(): listed = jnp.repeat(time_list.reshape(devices * LIST), 2)]
    all_to_all x2 -> x0, starting transfers between devices: 11.7 us -> none  [the longest x1 7.29 us: on_device(): lax.all_to_all(outgoing, ('src', 'att'), split_axis=0, concat_axis=0, til...]
    all_to_all x2 -> x0, waiting for transfers between devices: 9.94 us -> none  [the longest x1 9.94 us: on_device(): lax.all_to_all(returning, ('src', 'att'), split_axis=0, concat_axis=0, ti...]
  transfers between devices with their start and end apart: 2 -> 0, of which waited for: 1 -> 0; matrix products, arithmetic and copies ran while one was open for 1% -> 0% of each run, Pallas kernels for 0% -> 0%
where the time goes in v1:
time: 47.9 us; the launch traced here: 47.7 us
  Pallas kernels  41.3 us (86%)
  local copies, waits for them, and re-layouts  5.67 us (12%)
  between operations  0.68 us (1%)
    pallas_call x1, Pallas kernels, on_device(): pl.pallas_call(functools.partial(kernel, devices, n_att), out_shape=(jax....  41.3 us
    unnamed x12, local copies, waits for them, and re-layouts  2.6 us

profile of v1, /device:TPU:0, one launch (start us, length us, event | category | flops | bytes accessed | tf_op | source)
XLA Modules:
  0.0 47.7 jit_solution(1638377900770539251)
XLA Ops:
  0.6 0.0 copy-start.3
  0.6 0.7 %copy-done.3 = s32[32,1,4]{0,2,1:T(4,128)S(1)} copy-done((s32[32,1,4]{0,2,1:T(4,128)S(1)}, s32[32,1,4]{0,2,1:T(4,128)}, u32[]{:S(2)}) %copy-start.3) | copy-done | bytes 536
  1.3 0.1 copy.18
  1.4 0.1 reshape.50
  1.5 0.1 broadcast_in_dim.3
  1.6 0.7 %reshape_reshape.6.list_row = s32[1,256]{1,0:T(1,128)} reshape(s32[128,2]{1,0:T(8,128)S(1)} %broadcast_in_dim.3) | data formatting | bytes 2048 | tf_op jit(solution)/shard_map/reshape;reshape | solution.py:447
  2.3 0.7 %reshape_reshape.8.list_col = s32[256,1]{1,0:T(8,128)} reshape(s32[128,2]{1,0:T(8,128)S(1)} %broadcast_in_dim.3) | data formatting | bytes 2048 | tf_op jit(solution)/shard_map/reshape;reshape | solution.py:448
  3.0 41.3 %shard_map.156 = (f32[5,256]{1,0:T(8,128)}, f32[4,1024]{1,0:T(4,128)}, f32[32,1,128]{2,1,0:T(1,128)}, f32[1,8192]{1,0:T(1,128)}) custom-call(s32[1,4]{1,0:T(1,128)} %count_ref.1, f32[1,8192]{1,0:T(1,128)} %bitcast.12, f32[1,8192]{1,0:T(1,128)} %bitcast.13, f32[5,8192]{1,0:T(8,128)} %source_part.1, f32[4,8192]{1,0:T(4,128)} %attitude_part.1, ...), custom_call_target="tpu_custom_call" | custom-call | tf_op jit(solution)/shard_map/pallas_call | solution.py:398
  44.3 0.0 copy-start.2
  44.4 0.0 copy-start.1
  44.4 0.8 %slice_reduce_fusion = f32[32,64]{1,0:T(8,128)S(1)} fusion(f32[32,1,128]{2,1,0:T(1,128)} %get-tuple-element.10), kind=kLoop, calls=%fused_computation | loop fusion | bytes 16384 | tf_op jit(solution)/shard_map/slice | solution.py:450
  45.1 0.0 copy-start
  45.1 0.7 %reshape_squeeze.3 = f32[2048]{0:T(1024)} reshape(f32[32,64]{1,0:T(8,128)S(1)} %slice_reduce_fusion) | data formatting | bytes 16384 | tf_op jit(solution)/shard_map/reshape;squeeze | solution.py:450
  45.8 0.0 copy-done.2
  45.8 0.6 %copy.23 = f32[5,256]{1,0:T(8,128)} copy(f32[5,256]{1,0:T(8,128)S(1)} %copy-done.2) | data formatting | bytes 10240
  46.4 0.0 copy-done.1
  46.4 0.6 %copy.24 = f32[4,1024]{1,0:T(4,128)} copy(f32[4,1024]{1,0:T(4,128)S(1)} %copy-done.1) | data formatting | bytes 32768
  47.0 0.0 copy-done
  47.0 0.6 %copy.25 = f32[8192]{0:T(1024)} copy(f32[8192]{0:T(1024)S(1)} %bitcast.21) | data formatting | bytes 65536
Async XLA Ops:
  0.6 0.7 %copy-start.3 = (s32[32,1,4]{0,2,1:T(4,128)S(1)}, s32[32,1,4]{0,2,1:T(4,128)}, u32[]{:S(2)}) copy-start(s32[32,1,4]{0,2,1:T(4,128)} %param.25) | copy-start | bytes 1540
  44.3 1.5 %copy-start.2 = (f32[5,256]{1,0:T(8,128)S(1)}, f32[5,256]{1,0:T(8,128)}, u32[]{:S(2)}) copy-start(f32[5,256]{1,0:T(8,128)} %get-tuple-element.16) | copy-start | bytes 15364
  44.4 2.1 %copy-start.1 = (f32[4,1024]{1,0:T(4,128)S(1)}, f32[4,1024]{1,0:T(4,128)}, u32[]{:S(2)}) copy-start(f32[4,1024]{1,0:T(4,128)} %get-tuple-element.17) | copy-start | bytes 49156
  45.1 1.9 %copy-start = (f32[1,8192]{1,0:T(1,128)S(1)}, f32[1,8192]{1,0:T(1,128)}, u32[]{:S(2)}) copy-start(f32[1,8192]{1,0:T(1,128)} %get-tuple-element.11) | copy-start | bytes 98308

commit v2 on v1

--- a/solution.py
+++ b/solution.py
@@ -17,7 +17,7 @@
 HALF = 64
 WIN = 72
 LO = 64
-CHUNK = 1024
+CHUNK = 2048
 F32 = jnp.float32
 BF16 = jnp.bfloat16
 NT = (((1,), (1,)), ((), ()))
@@ -63,8 +63,7 @@
     obs_slot,
     obs_knot,
     obs_calib,
-    list_row,
-    list_col,
+    listing,
     source_out,
     attitude_out,
     calib_out,
@@ -200,6 +199,24 @@
     send_diag[...] = packed(acc[...]).reshape(devices, 8, 4 * HALF)
     cdiag_keep[...] = acc_cal[...]
 
+    blocks = KB_DEV * 2
+    sender = lax.broadcasted_iota(jnp.int32, (rows_a, devices), 0) // (2 * LIST)
+    sent = sender == lax.broadcasted_iota(jnp.int32, (rows_a, devices), 1)
+    entries = mm(
+        jnp.where(sent, F32(1.0), F32(0.0)).astype(BF16),
+        listing[...].astype(F32).astype(BF16),
+        NN,
+    )
+    slot = lax.rem(lax.broadcasted_iota(jnp.int32, (rows_a, LIST), 0) // 2, LIST)
+    own_slot = slot == lax.broadcasted_iota(jnp.int32, (rows_a, LIST), 1)
+    entry = jnp.sum(jnp.where(own_slot, entries, F32(0.0)), axis=1, keepdims=True)
+    tall = lax.broadcasted_iota(jnp.int32, (rows_a, 128), 1)
+    tall_half = lax.rem(lax.broadcasted_iota(jnp.int32, (rows_a, 128), 0), 2)
+    named = (tall - tall_half * KB_DEV).astype(F32) == entry
+    tall_hot = jnp.where(named, F32(1.0), F32(0.0))
+    scatter = tall_hot[:, 0:blocks].astype(BF16)
+    gather = tall_hot.T[0:blocks].astype(BF16)
+
     pl.semaphore_wait(barrier, devices - 1)
     spread(send_diag, recv_diag, 0)
 
@@ -251,8 +268,23 @@
             source_part[:, here] * per_obs[0:5], axis=0, keepdims=True
         )
 
+    acc_cal[...] = jnp.zeros_like(acc_cal)
+
+    def calib_step(step, carry):
+        here = pl.ds(pl.multiple_of(step * CHUNK, CHUNK), CHUNK)
+        scaled = weighted_all[:, here] * first_all[:, here]
+        group = obs_calib[:, here] // share
+        match = lax.broadcasted_iota(jnp.int32, (devices, CHUNK), 0) == group
+        chigh, clow = split2(jnp.where(match, scaled * calib_part[:, here], F32(0.0)))
+        calibs = calhot[:, here]
+        acc_cal[...] += mm(chigh, calibs, NT) + mm(clow, calibs, NT)
+        return carry
+
+    lax.fori_loop(0, count // CHUNK, calib_step, 0)
+    both = jnp.concatenate([acc_cal[...], cdiag_keep[...]], 1)
+    send_cal[...] = both[:, None, :]
+    spread(send_cal, recv_cal, 2)
     acc[...] = jnp.zeros_like(acc)
-    acc_cal[...] = jnp.zeros_like(acc_cal)
 
     def rhs_step(step, carry):
         here = pl.ds(pl.multiple_of(step * CHUNK, CHUNK), CHUNK)
@@ -263,40 +295,11 @@
         value = jnp.concatenate([lin * (scaled * att[c : c + 1]) for c in range(4)], 0)
         high, low = split2(value)
         acc[...] += mm(high, chosen, NT) + mm(low, chosen, NT)
-        group = obs_calib[:, here] // share
-        match = lax.broadcasted_iota(jnp.int32, (devices, CHUNK), 0) == group
-        chigh, clow = split2(jnp.where(match, scaled * calib_part[:, here], F32(0.0)))
-        calibs = calhot[:, here]
-        acc_cal[...] += mm(chigh, calibs, NT) + mm(clow, calibs, NT)
         return carry
 
     lax.fori_loop(0, count // CHUNK, rhs_step, 0)
     send_rhs[...] = packed(acc[...]).reshape(devices, 8, 4 * HALF)
     spread(send_rhs, recv_rhs, 1)
-    both = jnp.concatenate([acc_cal[...], cdiag_keep[...]], 1)
-    send_cal[...] = both[:, None, :]
-    spread(send_cal, recv_cal, 2)
-
-    blocks = KB_DEV * 2
-    wide = lax.broadcasted_iota(jnp.int32, (blocks, rows_a), 0)
-    wide_half = lax.rem(lax.broadcasted_iota(jnp.int32, (blocks, rows_a), 1), 2)
-    gather = jnp.where(wide == wide_half * KB_DEV + list_row[...], F32(1.0), F32(0.0)).astype(BF16)
-    tall = lax.broadcasted_iota(jnp.int32, (rows_a, blocks), 1)
-    tall_half = lax.rem(lax.broadcasted_iota(jnp.int32, (rows_a, blocks), 0), 2)
-    scatter = jnp.where(tall == tall_half * KB_DEV + list_col[...], F32(1.0), F32(0.0)).astype(BF16)
-
-    def owned(arrived):
-        high, middle, low = split3(arrived[...].reshape(rows_a, 4 * HALF))
-        return mm(gather, high, NN) + (mm(gather, middle, NN) + mm(gather, low, NN))
-
-    arrive(recv_diag, 0)
-    diag = owned(recv_diag)
-    arrive(recv_rhs, 1)
-    coef = owned(recv_rhs) / (diag + 1.0)
-    high, middle, low = split3(coef)
-    back = mm(scatter, high, NN) + (mm(scatter, middle, NN) + mm(scatter, low, NN))
-    send_ret[...] = back.reshape(devices, 8, 4 * HALF)
-    spread(send_ret, recv_ret, 3)
     arrive(recv_cal, 2)
     calsum = jnp.sum(recv_cal[...], axis=0)
     ratio = calsum / (pltpu.roll(calsum, LO, 1) + 1.0)
@@ -316,6 +319,19 @@
 
     pltpu.make_async_copy(send_calret, recv_calret.at[me], recv_sem.at[4]).start()
     lax.fori_loop(1, devices, one_cal, 0)
+
+    def owned(arrived):
+        high, middle, low = split3(arrived[...].reshape(rows_a, 4 * HALF))
+        return mm(gather, high, NN) + (mm(gather, middle, NN) + mm(gather, low, NN))
+
+    arrive(recv_diag, 0)
+    diag = owned(recv_diag)
+    arrive(recv_rhs, 1)
+    coef = owned(recv_rhs) / (diag + 1.0)
+    high, middle, low = split3(coef)
+    back = mm(scatter, high, NN) + (mm(scatter, middle, NN) + mm(scatter, low, NN))
+    send_ret[...] = back.reshape(devices, 8, 4 * HALF)
+    spread(send_ret, recv_ret, 3)
     for c in range(4):
         wide_rows = jnp.concatenate(
             [
@@ -331,7 +347,11 @@
 
     arrive(recv_calret, 4)
     calvals = recv_calret[...]
-    calib_out[...] = calvals
+    per_row = 128 // share
+    for block in range(NCAL // 128):
+        calib_out[:, block * 128 : (block + 1) * 128] = jnp.concatenate(
+            [calvals[block * per_row + k, :, 0:share] for k in range(per_row)], 1
+        )
     ctable = jnp.concatenate(split2(calvals.reshape(devices, 2 * LO)[:, 0:LO]), 0)
     arrive(recv_ret, 3)
     table = recv_ret[...].reshape(rows_a, 4 * HALF).T
@@ -368,6 +388,11 @@
     left(send_ret, 3)
     part = recv_calret.at[pl.ds(0, devices - 1)]
     pltpu.make_async_copy(part, part, send_sem.at[4]).wait()
+
+
+def hand_over(*refs):
+    for source, target in zip(refs[:4], refs[4:]):
+        target[...] = source[...]
 
 
 def on_device(n_src, n_att, *args):
@@ -390,20 +415,19 @@
     count = residual.shape[0]
     sources = count // OBS_TILE * SRC_TILE
     rows_a = devices * LIST * 2
-    listed = jnp.repeat(time_list.reshape(devices * LIST), 2)
     row = lambda x: x.reshape(1, count)
     vmem = pl.BlockSpec(memory_space=pltpu.VMEM)
     slab = pltpu.VMEM((devices, 8, 4 * HALF), F32)
     line = pltpu.VMEM((devices, 1, 2 * LO), F32)
-    source_update, attitude_update, calib, residual_out = pl.pallas_call(
+    results = pl.pallas_call(
         functools.partial(kernel, devices, n_att),
         out_shape=(
             jax.ShapeDtypeStruct((5, sources), F32),
             jax.ShapeDtypeStruct((4, KB_DEV * KNOT), F32),
-            jax.ShapeDtypeStruct((devices, 1, 2 * LO), F32),
+            jax.ShapeDtypeStruct((1, NCAL), F32),
             jax.ShapeDtypeStruct((1, count), F32),
         ),
-        in_specs=[pl.BlockSpec(memory_space=pltpu.SMEM)] + [vmem] * 13,
+        in_specs=[pl.BlockSpec(memory_space=pltpu.SMEM)] + [vmem] * 12,
         out_specs=(vmem,) * 4,
         scratch_shapes=[
             pltpu.VMEM((rows_a, count), BF16),
@@ -444,11 +468,15 @@
         row(obs_slot),
         row(obs_knot),
         row(obs_calib),
-        listed.reshape(1, rows_a),
-        listed.reshape(rows_a, 1),
+        time_list.reshape(devices, LIST),
     )
-    calib_update = calib[:, 0, 0 : NCAL // devices].reshape(NCAL)
-    return source_update, attitude_update, calib_update, residual_out.reshape(count)
+    source_update, attitude_update, calib_update, residual_out = pl.pallas_call(
+        hand_over,
+        out_shape=tuple(jax.ShapeDtypeStruct(r.shape, F32) for r in results),
+        in_specs=[vmem] * 4,
+        out_specs=(vmem,) * 4,
+    )(*results)
+    return source_update, attitude_update, calib_update.reshape(NCAL), residual_out.reshape(count)
 
 
 def solution(mesh):

time: 47.9 us -> 41.2 us (0.86)
  the two profiles are of different devices: /device:TPU:0 before, /device:TPU:27 now
where the time goes in v2:
time: 41.2 us; the launch traced here: 40.9 us
  Pallas kernels  38.9 us (94%)
  local copies, waits for them, and re-layouts  1.37 us (3%)
  between operations  0.65 us (2%)
    pallas_call x1, Pallas kernels, on_device(): pl.pallas_call(functools.partial(kernel, devices, n_att), out_shape=(jax....  37.4 us
    pallas_call x1, Pallas kernels, on_device(): pl.pallas_call(hand_over, out_shape=tuple((jax.ShapeDtypeStruct(r.shape,...  1.44 us

profile of v2, /device:TPU:27, one launch (start us, length us, event | category | flops | bytes accessed | tf_op | source)
XLA Modules:
  0.0 40.9 jit_solution(11927962007099135783)
XLA Ops:
  0.6 0.0 copy-start
  0.6 0.7 %copy-done = s32[32,1,4]{0,2,1:T(4,128)S(1)} copy-done((s32[32,1,4]{0,2,1:T(4,128)S(1)}, s32[32,1,4]{0,2,1:T(4,128)}, u32[]{:S(2)}) %copy-start) | copy-done | bytes 536
  1.3 0.7 %copy.17.listing = s32[32,4]{1,0:T(8,128)} copy(s32[32,4]{0,1:T(4,128)S(1)} %bitcast.21) | data formatting | bytes 1024 | tf_op jit(solution)/shard_map/reshape | solution.py:471
  2.0 37.4 %shard_map.156 = (f32[5,256]{1,0:T(8,128)}, f32[4,1024]{1,0:T(4,128)}, f32[1,2048]{1,0:T(1,128)}, f32[1,8192]{1,0:T(1,128)}) custom-call(s32[1,4]{1,0:T(1,128)} %count_ref.1, f32[1,8192]{1,0:T(1,128)} %bitcast.12, f32[1,8192]{1,0:T(1,128)} %bitcast.13, f32[5,8192]{1,0:T(8,128)} %source_part.1, f32[4,8192]{1,0:T(4,128)} %attitude_part.1, f32[1,8192]{1,0:T(1,128)} %bitcast.14, ...), custom_call_target="tpu_custom_call" | custom-call | tf_op jit(solution)/shard_map/pallas_call | solution.py:422
  39.4 1.4 %shard_map.157 = (f32[5,256]{1,0:T(8,128)}, f32[4,1024]{1,0:T(4,128)}, f32[1,2048]{1,0:T(1,128)}, f32[1,8192]{1,0:T(1,128)}) custom-call(f32[5,256]{1,0:T(8,128)} %get-tuple-element.12.refs_0_, f32[4,1024]{1,0:T(4,128)} %get-tuple-element.13.refs_1_, f32[1,2048]{1,0:T(1,128)} %get-tuple-element.14.refs_2_, f32[1,8192]{1,0:T(1,128)} %get-tuple-element.15.refs_3_), custom_call_target="tpu_custom_call" | custom-call | tf_op jit(solution)/shard_map/pallas_call | solution.py:473
Async XLA Ops:
  0.6 0.7 %copy-start = (s32[32,1,4]{0,2,1:T(4,128)S(1)}, s32[32,1,4]{0,2,1:T(4,128)}, u32[]{:S(2)}) copy-start(s32[32,1,4]{0,2,1:T(4,128)} %param.25) | copy-start | bytes 1540

commit v3 on v2

--- a/solution.py
+++ b/solution.py
@@ -111,7 +111,7 @@
         )
         return carry
 
-    lax.fori_loop(1, devices, greet, 0)
+    lax.fori_loop(1, devices, greet, 0, unroll=True)
 
     def spread(source, target, which):
         def one(step, carry):
@@ -127,7 +127,7 @@
             return carry
 
         pltpu.make_async_copy(source.at[me], target.at[me], recv_sem.at[which]).start()
-        lax.fori_loop(1, devices, one, 0)
+        lax.fori_loop(1, devices, one, 0, unroll=True)
 
     def arrive(target, which):
         pltpu.make_async_copy(target, target, recv_sem.at[which]).wait()
@@ -204,7 +204,7 @@
     sent = sender == lax.broadcasted_iota(jnp.int32, (rows_a, devices), 1)
     entries = mm(
         jnp.where(sent, F32(1.0), F32(0.0)).astype(BF16),
-        listing[...].astype(F32).astype(BF16),
+        listing[:, 0, :].astype(F32).astype(BF16),
         NN,
     )
     slot = lax.rem(lax.broadcasted_iota(jnp.int32, (rows_a, LIST), 0) // 2, LIST)
@@ -318,7 +318,7 @@
         return carry
 
     pltpu.make_async_copy(send_calret, recv_calret.at[me], recv_sem.at[4]).start()
-    lax.fori_loop(1, devices, one_cal, 0)
+    lax.fori_loop(1, devices, one_cal, 0, unroll=True)
 
     def owned(arrived):
         high, middle, low = split3(arrived[...].reshape(rows_a, 4 * HALF))
@@ -468,7 +468,7 @@
         row(obs_slot),
         row(obs_knot),
         row(obs_calib),
-        time_list.reshape(devices, LIST),
+        time_list,
     )
     source_update, attitude_update, calib_update, residual_out = pl.pallas_call(
         hand_over,

time: 41.2 us -> 40 us (0.971)
  the two profiles are of different devices: /device:TPU:27 before, /device:TPU:29 now
where the time goes in v3:
time: 40 us; the launch traced here: 39.8 us
  Pallas kernels  37.8 us (94%)
  local copies, waits for them, and re-layouts  1.37 us (3%)
  between operations  0.65 us (2%)
    pallas_call x1, Pallas kernels, on_device(): pl.pallas_call(functools.partial(kernel, devices, n_att), out_shape=(jax....  36.3 us
    pallas_call x1, Pallas kernels, on_device(): pl.pallas_call(hand_over, out_shape=tuple((jax.ShapeDtypeStruct(r.shape,...  1.44 us
    unnamed x3, local copies, waits for them, and re-layouts  1.37 us

profile of v3, /device:TPU:29, one launch (start us, length us, event | category | flops | bytes accessed | tf_op | source)
XLA Modules:
  0.0 39.8 jit_solution(13944877302369414940)
XLA Ops:
  0.6 0.0 copy-start
  0.6 0.7 %copy-done = s32[32,1,4]{0,2,1:T(4,128)S(1)} copy-done((s32[32,1,4]{0,2,1:T(4,128)S(1)}, s32[32,1,4]{0,2,1:T(4,128)}, u32[]{:S(2)}) %copy-start) | copy-done | bytes 536
  1.3 0.7 %copy.17.listing = s32[32,1,4]{2,1,0:T(1,128)} copy(s32[32,1,4]{0,2,1:T(4,128)S(1)} %copy-done) | data formatting | bytes 1024 | tf_op args[12]
  2.0 36.3 %shard_map.156 = (f32[5,256]{1,0:T(8,128)}, f32[4,1024]{1,0:T(4,128)}, f32[1,2048]{1,0:T(1,128)}, f32[1,8192]{1,0:T(1,128)}) custom-call(s32[1,4]{1,0:T(1,128)} %count_ref.1, f32[1,8192]{1,0:T(1,128)} %bitcast.11, f32[1,8192]{1,0:T(1,128)} %bitcast.12, f32[5,8192]{1,0:T(8,128)} %source_part.1, f32[4,8192]{1,0:T(4,128)} %attitude_part.1, f32[1,8192]{1,0:T(1,128)} %bitcast.13, ...), custom_call_target="tpu_custom_call" | custom-call | tf_op jit(solution)/shard_map/pallas_call | solution.py:422
  38.3 1.4 %shard_map.157 = (f32[5,256]{1,0:T(8,128)}, f32[4,1024]{1,0:T(4,128)}, f32[1,2048]{1,0:T(1,128)}, f32[1,8192]{1,0:T(1,128)}) custom-call(f32[5,256]{1,0:T(8,128)} %get-tuple-element.12.refs_0_, f32[4,1024]{1,0:T(4,128)} %get-tuple-element.13.refs_1_, f32[1,2048]{1,0:T(1,128)} %get-tuple-element.14.refs_2_, f32[1,8192]{1,0:T(1,128)} %get-tuple-element.15.refs_3_), custom_call_target="tpu_custom_call" | custom-call | tf_op jit(solution)/shard_map/pallas_call | solution.py:473
Async XLA Ops:
  0.6 0.7 %copy-start = (s32[32,1,4]{0,2,1:T(4,128)S(1)}, s32[32,1,4]{0,2,1:T(4,128)}, u32[]{:S(2)}) copy-start(s32[32,1,4]{0,2,1:T(4,128)} %param.25) | copy-start | bytes 1540
